TPU v7x, 256 devices: a whole 4x4x8 slice. The times are simulated.
256 devices in a mesh: section: 2 (over x_lo), ctx: 32 (over z, x_hi, core), head: 4 (over y).
Axes of the slice: x: 4 (x_hi: 2, x_lo: 2; x = x_hi * 2 + x_lo), y: 4, z: 8, core: 2. Of those that a mesh axis runs over, the one named last changes fastest.
Arguments:
- latent: bfloat16 [2, 4096, 576], P('section', 'ctx'), may hold values from -5 to 5
- queries: bfloat16 [2, 4096, 12288], P('section', 'ctx', 'head'), may hold values from -300 to 300
- w_key: bfloat16 [2, 512, 8192], P('section', None, 'head'), may hold values from -0.25 to 0.25
- w_value: bfloat16 [2, 512, 8192], P('section', None, 'head'), may hold values from -1 to 1
- w_next: bfloat16 [2, 8192, 576], P('section', 'head'), may hold values from -0.0625 to 0.0625
- segments: int32 [2, 4096], P('section', 'ctx'), may hold values from 0 to 3, never falling along the last dimension, each value on 1 to 2048 neighbouring positions
Outputs:
- attention: bfloat16 [2, 4096, 8192], P('section', 'ctx', 'head')
- next_latent: bfloat16 [2, 4096, 576], P('section', 'ctx')
Inputs may be any that keep to these rules, and one draw needn't show every extreme that they name: `segments`: document numbers never fall along a sequence; each sequence holds 4 documents, and one of them has half of its 4096 tokens.
All inputs are finite; a program needn't handle non-finite values.
Results may differ from a plain program's by a relative error of at most 0.017.
Values may be sent and summed in bfloat16 or wider, within the bound.
A program may use at most 192 MiB of HBM per device.

v0:
```python
import math

import jax
import jax.numpy as jnp
from jax import lax
from jax.sharding import PartitionSpec as P

KV_RANK = 512
ROPE = 64
NOPE = 128
VDIM = 128


def shifted(block, axis, distance):
    devices = range(lax.axis_size(axis))
    route = [((i - distance) % len(devices), i) for i in devices]
    return lax.ppermute(block, axis, route)


def masked_update(running, scores, query_pos, query_seg, key_seg, value_heads, form):
    running_max, denominator, weighted = running
    key_count = key_seg.shape[0]
    key_pos = jnp.arange(key_count, dtype=jnp.int32)
    allowed = (key_pos[None, :] <= query_pos[:, None]) & (key_seg[None, :] == query_seg[:, None])
    masked = jnp.where(allowed[None], scores, -jnp.inf)
    new_max = jnp.maximum(running_max, jnp.max(masked, axis=2))
    exponents = jnp.where(allowed[None], jnp.exp(scores - new_max[..., None]), 0.0)
    denominator = jnp.sum(exponents, axis=2)
    weighted = jnp.einsum(
        form, exponents.astype(jnp.bfloat16), value_heads, preferred_element_type=jnp.float32
    )
    return (new_max, denominator, weighted)


def attend_piece(
    running,
    query_nope,
    query_rope,
    query_pos,
    query_seg,
    keys_nope,
    values,
    rope_key,
    key_seg,
    score_scale,
):
    key_count = rope_key.shape[0]
    groups = query_nope.shape[1]
    key_heads = keys_nope.reshape(key_count, groups, NOPE)
    value_heads = values.reshape(key_count, groups, VDIM)
    scores = jnp.einsum("thd,nhd->htn", query_nope, key_heads, preferred_element_type=jnp.float32)
    scores = scores + jnp.einsum(
        "thr,nr->htn", query_rope, rope_key, preferred_element_type=jnp.float32
    )
    scores = scores * score_scale
    return masked_update(
        running, scores, query_pos, query_seg, key_seg, value_heads, "htn,nhv->htv"
    )


def normalize_rows(projected):
    compressed = projected[:, :KV_RANK]
    inverse = lax.rsqrt(jnp.mean(compressed * compressed, axis=1, keepdims=True) + 1e-06)
    return jnp.concatenate([compressed * inverse, projected[:, KV_RANK:]], axis=1).astype(
        jnp.bfloat16
    )


def local(latent, queries, w_key, w_value, w_next, segments):
    row_count = latent.shape[1]
    groups = w_key.shape[2] // NOPE
    score_scale = 1.0 / math.sqrt(NOPE + ROPE)
    query_heads = queries[0].reshape(row_count, groups, NOPE + ROPE)
    query_nope = query_heads[:, :, :NOPE]
    query_rope = query_heads[:, :, NOPE:]
    first_row = lax.axis_index("ctx") * row_count
    query_pos = first_row + jnp.arange(row_count, dtype=jnp.int32)
    query_seg = segments[0]
    start_max = jnp.full((groups, row_count), -1e30, jnp.float32)
    start_total = jnp.zeros((groups, row_count), jnp.float32)
    initial = (start_max, start_total, jnp.zeros((groups, row_count, VDIM), jnp.float32))
    key_weight = w_key[0]
    value_weight = w_value[0]

    def expand(latent_rows):
        compressed = latent_rows[:, :KV_RANK]
        keys_nope = jnp.dot(compressed, key_weight, preferred_element_type=jnp.float32).astype(
            jnp.bfloat16
        )
        values = jnp.dot(compressed, value_weight, preferred_element_type=jnp.float32).astype(
            jnp.bfloat16
        )
        return (keys_nope, values, latent_rows[:, KV_RANK:])

    latent_rows = lax.all_gather(latent[0], "ctx", axis=0, tiled=True)
    key_seg = lax.all_gather(query_seg, "ctx", axis=0, tiled=True)

    def attend_work(current):
        keys_nope, values, rope_key = expand(latent_rows)
        return attend_piece(
            current,
            query_nope,
            query_rope,
            query_pos,
            query_seg,
            keys_nope,
            values,
            rope_key,
            key_seg,
            score_scale,
        )

    needed = (jnp.int32(0) <= first_row + row_count - 1) & (key_seg[-1] >= query_seg[0])
    running_max, denominator, weighted = lax.cond(
        needed, attend_work, lambda current: current, initial
    )
    outputs = weighted / denominator[..., None]
    attention = (
        jnp.transpose(outputs, (1, 0, 2)).reshape(row_count, groups * VDIM).astype(jnp.bfloat16)
    )
    partial_rows = jnp.dot(attention, w_next[0], preferred_element_type=jnp.float32)
    summed_rows = lax.psum(partial_rows.astype(jnp.bfloat16), "head").astype(jnp.float32)
    arrived = shifted(summed_rows.astype(jnp.bfloat16), "section", 1).astype(summed_rows.dtype)
    next_latent = normalize_rows(arrived)
    return (attention[None], next_latent[None])


def solution(mesh):
    in_specs = (
        P("section", "ctx", None),
        P("section", "ctx", "head"),
        P("section", None, "head"),
        P("section", None, "head"),
        P("section", "head", None),
        P("section", "ctx"),
    )
    out_specs = (P("section", "ctx", "head"), P("section", "ctx", None))
    return jax.shard_map(local, mesh=mesh, in_specs=in_specs, out_specs=out_specs, check_vma=False)
```

profile of v0, /device:TPU:160, one launch (start us, length us, event | category | flops | bytes accessed | tf_op | source)
XLA Modules:
  0.0 263.8 jit_solution(1937210114975572400)
XLA Ops:
  7.2 0.0 copy-start
  7.2 0.0 all-gather.4.cloned.1.call-start
  7.2 0.7 all-gather.4.cloned.1.call-update
  7.9 0.0 all-reduce.2.cloned.1.call-start
  8.0 37.7 %all-gather = s32[1,4096]{1,0:T(1,128)S(1)} all-gather(s32[1,128]{1,0:T(1,128)} %param.13), channel_id=2, replica_groups=mesh['section'=2,'ctx'=32,'head'=4] {'ctx'}, dimensions={1}, use_global_device_ids=true | all-gather | bytes 16896 | tf_op jit(solution)/shard_map/all_gather | solution.py:96
  45.7 0.6 slice.43
  47.6 52.0 %all-gather.4.cloned.1.call-done = bf16[1,4096,576]{1,2,0:T(8,128)(2,1)} async-done(((bf16[1,128,576]{1,2,0:T(8,128)(2,1)}), bf16[1,4096,576]{1,2,0:T(8,128)(2,1)}) %all-gather.4.cloned.1.call-update) | async-done | bytes 4718608 | tf_op jit(solution)/shard_map/all_gather | solution.py:95
  99.5 103.7 %conditional.1 = (f32[16,128]{1,0:T(8,128)S(1)}, f32[16,128,128]{1,2,0:T(8,128)S(1)}) conditional(s32[]{:T(128)} %convert_element_type.49, () %tuple.19, (s32[]{:T(128)}, s32[128]{0:T(128)S(1)}, s32[4096]{0:T(1024)S(1)}, s32[1,128]{1,0:T(1,128)}, bf16[4096,576]{0,1:T(8,128)(2,1)}, /*index=5*/bf16[1,512,2048]{2,1,0:T(8,128)(2,1)}, ...), branch_computations={%region_0.0_spmd, %region_1.4_spmd} | conditional | flops 22650812416 | bytes 261951568 | solution.py:114
  99.5 14.8 %convolution_convert_fusion.1 = bf16[4096,2048]{0,1:T(8,128)(2,1)} fusion(bf16[4096,576]{0,1:T(8,128)(2,1)} %get-tuple-element.44, bf16[1,512,2048]{2,1,0:T(8,128)(2,1)} %get-tuple-element.57), kind=kOutput, calls=%fused_computation.11 | convolution fusion | flops 8598323200 | bytes 23068672 | tf_op jit(solution)/shard_map/cond/branch_1_fun/dot_general | solution.py:87
  114.3 1.5 copy.20
  115.9 0.0 copy-start.2
  115.9 17.1 %fusion.13 = f32[16,4096,128]{2,1,0:T(8,128)} fusion(bf16[4096,16,128]{0,2,1:T(8,128)(2,1)} %bitcast.42, bf16[128,16,192]{0,2,1:T(8,128)(2,1)S(1)} %bitcast.43), kind=kOutput, calls=%fused_computation.18 | convolution fusion | flops 2147483648 | bytes 50855936 | tf_op jit(solution)/shard_map/cond/branch_1_fun/thd,nhd->htn/dot_general | solution.py:51
  132.9 0.0 copy-done.2
  132.9 1.9 fusion.12
  134.8 0.0 copy-start.3
  134.8 21.8 %select_reduce_fusion = (f32[16,128]{1,0:T(8,128)S(1)}, f32[16,128,4096]{1,2,0:T(8,128)}) fusion(pred[128,4096]{0,1:T(8,128)(4,1)S(1)} %fusion.12, bf16[128,16,192]{0,2,1:T(8,128)(2,1)S(1)} %bitcast.44, bf16[4096,576]{0,1:T(8,128)(2,1)} %get-tuple-element.44, f32[16,4096,128]{2,1,0:T(8,128)} %fusion.13), kind=kOutput, calls=%fused_computation.3 | convolution fusion | flops 1107294208 | bytes 68427776 | tf_op jit(solution)/shard_map/cond/branch_1_fun/thr,nr->htn/dot_general | solution.py:52
  156.6 0.0 copy-done.3
  156.6 14.7 %convolution_convert_fusion = bf16[4096,2048]{0,1:T(8,128)(2,1)} fusion(bf16[4096,576]{0,1:T(8,128)(2,1)} %get-tuple-element.44, bf16[1,512,2048]{2,1,0:T(8,128)(2,1)S(1)} %copy-done.3), kind=kOutput, calls=%fused_computation.10 | convolution fusion | flops 8598323200 | bytes 23068672 | tf_op jit(solution)/shard_map/cond/branch_1_fun/dot_general | solution.py:90
  171.3 18.0 %fusion.3 = f32[16,128,128]{1,2,0:T(8,128)S(1)} fusion(bf16[4096,16,128]{0,2,1:T(8,128)(2,1)} %bitcast.51, f32[16,128,4096]{1,2,0:T(8,128)} %get-tuple-element.72, f32[16,128]{1,0:T(8,128)S(1)} %broadcast_maximum_fusion, pred[128,4096]{0,1:T(8,128)(4,1)S(1)} %fusion.12), kind=kOutput, calls=%fused_computation.6 | convolution fusion | flops 2172649472 | bytes 51912704 | tf_op jit(solution)/shard_map/cond | solution.py:114
  189.3 13.6 %fusion.2 = f32[16,128]{1,0:T(8,128)S(1)} fusion(f32[16,128,4096]{1,2,0:T(8,128)} %get-tuple-element.72, f32[16,128]{1,0:T(8,128)S(1)} %broadcast_maximum_fusion, pred[128,4096]{0,1:T(8,128)(4,1)S(1)} %fusion.12), kind=kLoop, calls=%fused_computation.5 | loop fusion | flops 25163776 | bytes 34095104 | tf_op jit(solution)/shard_map/cond/branch_1_fun/reduce_sum | solution.py:28
  203.2 0.1 divide_convert_fusion
  203.3 0.0 copy-start.1
  203.3 0.8 copy-done.1
  204.1 0.0 copy-done
  204.1 1.4 fusion.21
  205.6 0.0 all-reduce.2.cloned.1.call-update
  205.6 45.2 %all-reduce.2.cloned.1.call-done = bf16[128,576]{0,1:T(8,128)(2,1)} async-done(((bf16[128,576]{0,1:T(8,128)(2,1)}), bf16[128,576]{0,1:T(8,128)(2,1)}) %all-reduce.2.cloned.1.call-update) | async-done | bytes 147472 | tf_op jit(solution)/shard_map/psum | solution.py:122
  250.8 1.5 collective-permute-start
  252.2 2.0 copy.22
  254.3 1.8 collective-permute-done
  256.1 0.1 fusion.24
  256.3 0.7 pad_maximum_fusion
  (6 shorter events, 0.0 us)
Async XLA Ops:
  7.2 197.0 %copy-start = (bf16[1,2048,576]{1,2,0:T(8,128)(2,1)S(1)}, bf16[1,2048,576]{1,2,0:T(8,128)(2,1)}, u32[]{:S(2)}) copy-start(bf16[1,2048,576]{1,2,0:T(8,128)(2,1)} %param.12) | copy-start | bytes 7077892
  7.2 92.3 %all-gather.4.cloned.1.call-start = ((), (), s32[]{:S(2)}) async-start(), calls=%async_computation.1 | async-start | bytes 4866048 | tf_op jit(solution)/shard_map/all_gather | solution.py:95
  7.9 242.9 %all-reduce.2.cloned.1.call-start = ((), (), s32[]{:S(2)}) async-start(), calls=%async_computation | async-start | bytes 294912 | tf_op jit(solution)/shard_map/psum | solution.py:122
  115.9 17.1 %copy-start.2 = (s32[1,128]{1,0:T(1,128)S(1)}, s32[1,128]{1,0:T(1,128)}, u32[]{:S(2)}) copy-start(s32[1,128]{1,0:T(1,128)} %get-tuple-element.43) | copy-start | bytes 1540 | tf_op jit(solution)/shard_map/cond
  134.8 21.8 %copy-start.3 = (bf16[1,512,2048]{2,1,0:T(8,128)(2,1)S(1)}, bf16[1,512,2048]{2,1,0:T(8,128)(2,1)}, u32[]{:S(2)}) copy-start(bf16[1,512,2048]{2,1,0:T(8,128)(2,1)} %get-tuple-element.59) | copy-start | bytes 6291460 | tf_op jit(solution)/shard_map/cond
  203.3 0.8 copy-start.1
  250.8 5.4 %collective-permute-start = (bf16[128,576]{0,1:T(8,128)(2,1)}, bf16[128,576]{0,1:T(8,128)(2,1)S(1)}, u32[]{:S(2)}, u32[]{:S(2)}) collective-permute-start(bf16[128,576]{0,1:T(8,128)(2,1)} %all-reduce.2.cloned.1.call-done), channel_id=1, source_target_pairs={{128,0},{0,128},{129,1},{1,129},{130,2},{2,130},{131,3},{3,131},{1... | collective-permute-start | bytes 442376 | tf_op jit(solution)/shard_map/ppermute | solution.py:17
Sparse Core Ops, SparseCore 0:
  10.6 88.8 all-gather.3
  205.7 45.0 all-reduce.1
where the time goes:
time: 266 us; the launch traced here: 264 us
  waiting for transfers between devices  99.7 us (37%)
  matrix products  87.8 us (33%)
  blocking collectives  37.7 us (14%)
  other arithmetic  16.4 us (6%)
  between operations  15.4 us (6%)
  local copies, waits for them, and re-layouts  4.94 us (2%)
    all_gather x1, waiting for transfers between devices, local(): latent_rows = lax.all_gather(latent[0], 'ctx', axis=0, tiled=True)  52 us
    psum x1, waiting for transfers between devices, local(): lax.psum(partial_rows.astype(jnp.bfloat16), 'head').astype(jnp.float32)  45.2 us
    all_gather x1, blocking collectives, local(): key_seg = lax.all_gather(query_seg, 'ctx', axis=0, tiled=True)  37.7 us
    dot_general x1, matrix products, attend_piece(): jnp.einsum('thr,nr->htn', query_rope, rope_key, preferred_element_type=jn...  21.8 us
    cond x1, matrix products, local(): lax.cond(needed, attend_work, lambda current: current, initial)  18 us
    dot_general x1, matrix products, attend_piece(): jnp.einsum('thd,nhd->htn', query_nope, key_heads, preferred_element_type=...  17.1 us
    dot_general x1, matrix products, expand(): jnp.dot(compressed, key_weight, preferred_element_type=jnp.float32)  14.8 us
    dot_general x1, matrix products, expand(): jnp.dot(compressed, value_weight, preferred_element_type=jnp.float32)  14.7 us
  transfers between devices with their start and end apart: 3, of which 3 were waited for; matrix products, arithmetic and copies ran while one was open for 1% of the time, Pallas kernels for 0%

commit v1 on v0

v1 whole, which is shorter than its diff:
```python
import math

import jax
import jax.numpy as jnp
from jax import lax
from jax.experimental import pallas as pl
from jax.experimental.pallas import tpu as pltpu
from jax.sharding import PartitionSpec as P

MESH = pl.DeviceIdType.MESH
RANK = 512
ROPE = 64
NOPE = 128
VDIM = 128
LAT = 576
WIDE = 640
ROWS = 128
QUARTER = 32
CHUNK = 512
CHUNKS = 4
KEYS = ROWS + CHUNK * CHUNKS
DOCS = 4
BIG = float(2**30)
FOLD = math.log2(math.e) / math.sqrt(NOPE + ROPE)
NT = (((1,), (1,)), ((), ()))
F32 = jnp.float32
BF16 = jnp.bfloat16
X0, Z1A, Z1B, SIB, Z, YL, YR, FL, FR, CORE, RS, NL, SEMS = 0, 1, 2, 3, 4, 8, 12, 16, 20, 24, 28, 31, 35


def make_kernel(planes, heads):
    rows_all = heads * ROWS
    group = 4
    grow = group * ROWS
    groups = heads // group

    def kernel(lat_hbm, q_hbm, wk_hbm, wv_hbm, wn_hbm, seg_hbm, att_hbm, next_hbm,
               lat, seg, qv, wk, wv, wn, qx, kx, xp, sib, sc, top, ob, att, proj, part, rsb, nlp, nlb,
               ls, ss, rs):
        s = lax.axis_index("section")
        t = lax.axis_index("ctx")
        y = lax.axis_index("head")
        z, xh, c = t // 4, (t // 2) % 2, t % 2

        def at(zz, xx, cc, yy, section=s):
            return {"section": section, "ctx": zz * 4 + xx * 2 + cc, "head": yy}

        up, down = (z + 1) % planes, (z + planes - 1) % planes
        right, left, across = (y + 1) % 4, (y + 3) % 4, (y + 2) % 4

        def load(i, src, dst):
            return pltpu.make_async_copy(src, dst, ls.at[i])

        loads = [
            load(0, lat_hbm.at[0], lat),
            load(1, seg_hbm, seg),
            load(2, q_hbm.at[0], qv),
            load(3, wk_hbm.at[0], wk),
            load(4, wv_hbm.at[0], wv),
            load(5, wn_hbm.at[0], wn),
        ]
        for one in loads:
            one.start()

        barrier = pltpu.get_barrier_semaphore()
        peers = [
            at(down, xh, c, y), at(down, 1 - xh, c, y), at(z, 1 - xh, c, y), at(z, xh, 1 - c, y),
            at(z, xh, c, right), at(z, xh, c, left), at(z, xh, c, across),
        ] + [at(z, xh, c, (y + d) % 4, 1 - s) for d in range(4)]
        for peer in peers:
            pl.semaphore_signal(barrier, inc=1, device_id=peer, device_id_type=MESH)

        def remote(i, src, dst, peer):
            return pltpu.make_async_remote_copy(
                src_ref=src, dst_ref=dst, send_sem=ss.at[i], recv_sem=rs.at[i], device_id=peer, device_id_type=MESH
            )

        sent = []

        def send(i, src, dst, peer):
            one = remote(i, src, dst, peer)
            one.start()
            sent.append(one)

        def arrive(i, dst):
            remote(i, dst, dst, at(z, xh, c, right)).wait_recv()

        def rows(start, size):
            return kx.at[pl.ds(pl.multiple_of(start, QUARTER), size)]

        def pair(k, yy):
            return rows(ROWS + CHUNK * (k - 1) + c * 256 + yy * 64, 64)

        def piece(k, yy, xx):
            return rows(ROWS + CHUNK * (k - 1) + c * 256 + yy * 64 + xx * QUARTER, QUARTER)

        def half(k, cc):
            return rows(ROWS + CHUNK * (k - 1) + cc * 256, 256)

        loads[0].wait()
        loads[1].wait()
        lane = lax.broadcasted_iota(jnp.int32, (ROWS, 128), 1)
        doc = jnp.broadcast_to(seg[...].astype(F32), (ROWS, 128)).T
        slot = (lane - ROPE).astype(F32)
        in_slot = (lane >= ROPE) & (lane < ROPE + DOCS)
        mine = in_slot & (slot == doc)
        kx[0:ROWS, 0:RANK] = lat[:, 0:RANK]
        rope = jnp.concatenate([lat[:, RANK:LAT].astype(F32), jnp.zeros((ROWS, ROPE), F32)], axis=1)
        kx[0:ROWS, RANK:WIDE] = jnp.where(mine, 1.0, rope).astype(BF16)
        q_mark = jnp.where(in_slot & (slot != doc), -BIG, 0.0)
        pl.semaphore_wait(barrier, len(peers))

        own = rows(y * QUARTER, QUARTER)
        send(Z1A, own, piece(1, y, xh), at(up, xh, c, y))
        send(Z1B, own, piece(1, y, xh), at(up, 1 - xh, c, y))
        send(X0, own, xp, at(z, 1 - xh, c, y))
        send(SIB, kx.at[pl.ds(0, ROWS)], sib, at(z, xh, 1 - c, y))

        def stage_z(k):
            if k == 1:
                arrive(Z1A, piece(1, y, xh))
                arrive(Z1B, piece(1, y, 1 - xh))
            else:
                arrive(Z + k - 1, pair(k, y))
            start = pl.multiple_of(ROWS + CHUNK * (k - 1) + c * 256 + y * 64, 64)

            @pl.when(z < k)
            def _():
                mark = lax.broadcasted_iota(jnp.int32, (64, 128), 1)
                kx[pl.ds(start, 64), RANK:WIDE] = jnp.where(
                    (mark >= ROPE) & (mark < ROPE + DOCS), 1.0, 0.0
                ).astype(BF16)

            if k == CHUNKS:
                arrive(X0, xp)

                @pl.when(xh == 1)
                def _():
                    kx[pl.ds(start, QUARTER), :] = xp[...]
            else:
                send(Z + k, pair(k, y), pair(k + 1, y), at(up, xh, c, y))
            send(YL + k - 1, pair(k, y), pair(k, y), at(z, xh, c, right))
            send(YR + k - 1, pair(k, y), pair(k, y), at(z, xh, c, left))

        def stage_y(k):
            arrive(YL + k - 1, pair(k, left))
            send(FL + k - 1, piece(k, left, 0), piece(k, left, 0), at(z, xh, c, right))
            arrive(YR + k - 1, pair(k, right))
            send(FR + k - 1, piece(k, right, 1), piece(k, right, 1), at(z, xh, c, left))

        def stage_f(k):
            arrive(FL + k - 1, piece(k, across, 0))
            arrive(FR + k - 1, piece(k, across, 1))
            send(CORE + k - 1, half(k, c), half(k, c), at(z, xh, 1 - c, y))

        def stage_c(k):
            arrive(CORE + k - 1, half(k, 1 - c))
            if k == CHUNKS:
                arrive(SIB, sib)

                @pl.when(c == 1)
                def _():
                    for yy in range(4):
                        start = pl.multiple_of(ROWS + CHUNK * (k - 1) + yy * 64 + xh * QUARTER, QUARTER)
                        kx[pl.ds(start, QUARTER), :] = sib[yy * QUARTER : (yy + 1) * QUARTER, :]

        def queries(p):
            base = 3 * 128 * p
            one = qv[:, base : base + 128]
            two = qv[:, base + 128 : base + 256].astype(F32)
            three = qv[:, base + 256 : base + 384].astype(F32)
            two_turned = pltpu.roll(two, 64, 1)
            three_turned = pltpu.roll(three, 64, 1)
            second = jnp.where(lane < 64, two_turned, three_turned).astype(BF16)
            for h, nope, pos in ((2 * p, one, two), (2 * p + 1, second, three_turned)):
                absorbed = lax.dot_general(
                    nope, wk[:, h * NOPE : (h + 1) * NOPE], NT, preferred_element_type=F32
                )
                qx[h * ROWS : (h + 1) * ROWS, 0:RANK] = (absorbed * FOLD).astype(BF16)
                qx[h * ROWS : (h + 1) * ROWS, RANK:WIDE] = jnp.where(lane < ROPE, pos * FOLD, q_mark).astype(BF16)

        def lane_max(scores):
            best = scores[:, 0:128]
            for i in range(1, scores.shape[1] // 128):
                best = jnp.maximum(best, scores[:, i * 128 : (i + 1) * 128])
            return best

        def diagonal():
            later = lax.broadcasted_iota(jnp.int32, (ROWS, ROWS), 1) > lax.broadcasted_iota(
                jnp.int32, (ROWS, ROWS), 0
            )
            mask = jnp.concatenate([jnp.where(later, -2.0 * BIG, 0.0)] * group, axis=0)
            for g in range(groups):
                r = slice(g * grow, (g + 1) * grow)
                scores = lax.dot_general(qx[r, :], kx[0:ROWS, :], NT, preferred_element_type=F32)
                scores = scores + mask
                sc[r, 0:ROWS] = scores
                top[r, :] = scores

        def chunk_scores(k, g):
            r = slice(g * grow, (g + 1) * grow)
            first = ROWS + CHUNK * (k - 1)
            scores = lax.dot_general(qx[r, :], kx[first : first + CHUNK, :], NT, preferred_element_type=F32)
            sc[r, first : first + CHUNK] = scores
            top[r, :] = jnp.maximum(top[r, :], lane_max(scores))

        def lane_sum(weights):
            total = weights[:, 0:128]
            for i in range(1, weights.shape[1] // 128):
                total = total + weights[:, i * 128 : (i + 1) * 128]
            return total

        def finish(g):
            r = slice(g * grow, (g + 1) * grow)
            first = KEYS - CHUNK
            last = lax.dot_general(qx[r, :], kx[first:KEYS, :], NT, preferred_element_type=F32)
            high = jnp.max(jnp.maximum(top[r, :], lane_max(last)), axis=1, keepdims=True)
            early = jnp.exp2(sc[r, :] - high)
            late = jnp.exp2(last - high)
            total = jnp.sum(lane_sum(early) + lane_sum(late), axis=1, keepdims=True)
            mixed = jnp.dot(early.astype(BF16), kx[0:first, 0:RANK], preferred_element_type=F32)
            mixed = mixed + jnp.dot(late.astype(BF16), kx[first:KEYS, 0:RANK], preferred_element_type=F32)
            ob[r, :] = (mixed * (1.0 / total)).astype(BF16)
            for h in range(g * group, (g + 1) * group):
                att[:, h * VDIM : (h + 1) * VDIM] = jnp.dot(
                    ob[h * ROWS : (h + 1) * ROWS, :],
                    wv[:, h * VDIM : (h + 1) * VDIM],
                    preferred_element_type=F32,
                ).astype(BF16)

        half_pairs = heads // 4
        loads[2].wait()
        loads[3].wait()
        for p in range(half_pairs):
            queries(p)
        stage_z(1)
        for p in range(half_pairs, 2 * half_pairs):
            queries(p)
        diagonal()
        stage_y(1)
        stage_z(2)
        stage_f(1)
        stage_y(2)
        stage_z(3)
        stage_c(1)
        for g in range(groups):
            chunk_scores(1, g)
            if g == 1:
                stage_f(2)
        stage_y(3)
        stage_z(4)
        stage_c(2)
        for g in range(groups):
            chunk_scores(2, g)
            if g == 1:
                stage_f(3)
        stage_y(4)
        stage_c(3)
        for g in range(groups):
            chunk_scores(3, g)
            if g == 1:
                stage_f(4)
        stage_c(4)
        loads[4].wait()
        for g in range(groups):
            finish(g)
        store = pltpu.make_async_copy(att, att_hbm.at[0], ls.at[6])
        store.start()
        loads[5].wait()
        proj[...] = jnp.dot(att[...], wn[...], preferred_element_type=F32)
        part[...] = proj[...].astype(BF16)
        for d in range(1, 4):
            to = (y + d) % 4
            send(
                RS + d - 1,
                part.at[pl.ds(pl.multiple_of(to * QUARTER, QUARTER), QUARTER)],
                rsb.at[d - 1],
                at(z, xh, c, to),
            )
        total = proj[pl.ds(pl.multiple_of(y * QUARTER, QUARTER), QUARTER), :]
        for d in range(1, 4):
            arrive(RS + d - 1, rsb.at[d - 1])
            total = total + rsb[d - 1].astype(F32)
        low = total[:, 0:RANK]
        inverse = lax.rsqrt(jnp.sum(low * low, axis=1, keepdims=True) * (1.0 / RANK) + 1e-06)
        nlp[:, 0:RANK] = (low * inverse).astype(BF16)
        nlp[:, RANK:LAT] = total[:, RANK:LAT].astype(BF16)

        def block(yy):
            return nlb.at[pl.ds(pl.multiple_of(yy * QUARTER, QUARTER), QUARTER)]

        for d in range(4):
            send(NL + d, nlp, block(y), at(z, xh, c, (y + d) % 4, 1 - s))
        for d in range(4):
            arrive(NL + d, block((y + 4 - d) % 4))
        out = pltpu.make_async_copy(nlb, next_hbm.at[0], ls.at[7])
        out.start()
        for one in sent:
            one.wait_send()
        store.wait()
        out.wait()

    def call(latent, queries, w_key, w_value, w_next, segments):
        return pl.pallas_call(
            kernel,
            out_shape=(
                jax.ShapeDtypeStruct((1, ROWS, heads * VDIM), BF16),
                jax.ShapeDtypeStruct((1, ROWS, LAT), BF16),
            ),
            in_specs=[pl.BlockSpec(memory_space=pl.ANY)] * 6,
            out_specs=[pl.BlockSpec(memory_space=pl.ANY)] * 2,
            scratch_shapes=[
                pltpu.VMEM((ROWS, LAT), BF16),
                pltpu.VMEM((1, ROWS), jnp.int32),
                pltpu.VMEM((ROWS, heads * (NOPE + ROPE)), BF16),
                pltpu.VMEM((RANK, heads * NOPE), BF16),
                pltpu.VMEM((RANK, heads * VDIM), BF16),
                pltpu.VMEM((heads * VDIM, LAT), BF16),
                pltpu.VMEM((rows_all, WIDE), BF16),
                pltpu.VMEM((KEYS, WIDE), BF16),
                pltpu.VMEM((QUARTER, WIDE), BF16),
                pltpu.VMEM((ROWS, WIDE), BF16),
                pltpu.VMEM((rows_all, KEYS - CHUNK), F32),
                pltpu.VMEM((rows_all, 128), F32),
                pltpu.VMEM((rows_all, RANK), BF16),
                pltpu.VMEM((ROWS, heads * VDIM), BF16),
                pltpu.VMEM((ROWS, LAT), F32),
                pltpu.VMEM((ROWS, LAT), BF16),
                pltpu.VMEM((3, QUARTER, LAT), BF16),
                pltpu.VMEM((QUARTER, LAT), BF16),
                pltpu.VMEM((ROWS, LAT), BF16),
                pltpu.SemaphoreType.DMA((8,)),
                pltpu.SemaphoreType.DMA((SEMS,)),
                pltpu.SemaphoreType.DMA((SEMS,)),
            ],
            compiler_params=pltpu.CompilerParams(
                collective_id=0, has_side_effects=True, vmem_limit_bytes=58 * 2**20
            ),
            name="attend",
        )(latent, queries, w_key, w_value, w_next, segments)

    return call


def solution(mesh):
    planes = mesh.shape["ctx"] // 4

    def local(latent, queries, w_key, w_value, w_next, segments):
        return make_kernel(planes, w_key.shape[2] // NOPE)(latent, queries, w_key, w_value, w_next, segments)

    in_specs = (
        P("section", "ctx", None),
        P("section", "ctx", "head"),
        P("section", None, "head"),
        P("section", None, "head"),
        P("section", "head", None),
        P("section", "ctx"),
    )
    out_specs = (P("section", "ctx", "head"), P("section", "ctx", None))
    return jax.shard_map(local, mesh=mesh, in_specs=in_specs, out_specs=out_specs, check_vma=False)
```

time: 266 us -> 70.2 us (0.26)
  the two profiles are of different devices: /device:TPU:160 before, /device:TPU:2 now
where the time goes in v1:
time: 70.2 us; the launch traced here: 69.9 us
  Pallas kernels  59.6 us (85%)
  local copies, waits for them, and re-layouts  9.63 us (14%)
    pallas_call x1, Pallas kernels, call(): pl.pallas_call(kernel, out_shape=(jax.ShapeDtypeStruct((1, ROWS, heads *...  59.6 us
    unnamed x3, local copies, waits for them, and re-layouts  7.93 us
    pallas_call x1, local copies, waits for them, and re-layouts, call(): pl.pallas_call(kernel, out_shape=(jax.ShapeDtypeStruct((1, ROWS, heads *...  1.7 us

profile of v1, /device:TPU:2, one launch (start us, length us, event | category | flops | bytes accessed | tf_op | source)
XLA Modules:
  0.0 69.9 jit_solution(13179416871595469189)
XLA Ops:
  0.6 1.7 %copy.8.lat_hbm = bf16[1,128,576]{2,1,0:T(8,128)(2,1)} copy(bf16[1,128,576]{1,2,0:T(8,128)(2,1)} %param.6) | data formatting | bytes 294912 | tf_op args[0]
  2.3 4.3 %copy.9.wn_hbm = bf16[1,2048,576]{2,1,0:T(8,128)(2,1)} copy(bf16[1,2048,576]{1,2,0:T(8,128)(2,1)} %param.10) | data formatting | bytes 4718592 | tf_op args[4]
  6.7 59.6 %attend.1 = (bf16[1,128,2048]{2,1,0:T(8,128)(2,1)}, bf16[1,128,576]{2,1,0:T(8,128)(2,1)}) custom-call(bf16[1,128,576]{2,1,0:T(8,128)(2,1)} %copy.8.lat_hbm, bf16[1,128,3072]{2,1,0:T(8,128)(2,1)} %q_hbm.1, bf16[1,512,2048]{2,1,0:T(8,128)(2,1)} %wk_hbm.1, bf16[1,512,2048]{2,1,0:T(8,128)(2,1)} %wv_hbm.1, bf16[1,2048,576]{2,1,0:T(8,128)(2,1)} %copy.9.wn_hbm, ...), custom_call_target="tpu_custom_call" | custom-call | tf_op jit(solution)/shard_map/attend/pallas_call | solution.py:304
  66.3 1.7 %copy.10 = bf16[1,128,576]{1,2,0:T(8,128)(2,1)} copy(bf16[1,128,576]{2,1,0:T(8,128)(2,1)} %get-tuple-element.3) | data formatting | bytes 294912 | tf_op jit(solution)/shard_map/attend/pallas_call | solution.py:304
  68.0 1.9 %copy.12 = bf16[1,128,2048]{2,1,0:T(8,128)(2,1)} copy(bf16[1,128,2048]{2,1,0:T(8,128)(2,1)} %get-tuple-element.6) | data formatting | bytes 1048576

commit v2 on v1

v2 whole, which is shorter than its diff:
```python
import math

import jax
import jax.numpy as jnp
from jax import lax
from jax.experimental import pallas as pl
from jax.experimental.pallas import tpu as pltpu
from jax.sharding import PartitionSpec as P

MESH = pl.DeviceIdType.MESH
RANK = 512
ROPE = 64
NOPE = 128
VDIM = 128
LAT = 576
WIDE = 640
ROWS = 128
QUARTER = 32
HALF = 16
CHUNK = 512
CHUNKS = 4
KEYS = ROWS + CHUNK * CHUNKS
DOCS = 4
BIG = float(2**30)
FOLD = math.log2(math.e) / math.sqrt(NOPE + ROPE)
NT = (((1,), (1,)), ((), ()))
F32 = jnp.float32
BF16 = jnp.bfloat16
SEMS = 72
ROUTES = ('', 'X', 'D', 'X', 'S')
PLAN = (
    ("q", 0), ("q", 1), ("q", 2), ("q", 3), ("q", 4), ("z", 1), ("q", 5), ("q", 6), ("q", 7), ("z", 2),
    ("diag", 0), ("diag", 1), ("diag", 2), ("diag", 3), ("xs", 1, 1), ("xs", 1, 3), ("z", 3), ("xs", 1, 2),
    ("ca", 1), ("x", 2), ("z", 4), ("ca", 2), ("xs", 3, 1), ("xs", 3, 3), ("xs", 3, 2), ("ca", 3), ("cb", 1),
    ("cb", 2), ("done", 1), ("qk", 1, 0), ("qk", 1, 1), ("done", 2), ("qk", 1, 2), ("ca", 4), ("qk", 1, 3),
    ("qk", 2, 0), ("cb", 4), ("qk", 2, 1), ("qk", 2, 2), ("qk", 2, 3), ("cb", 3), ("done", 3), ("qk", 3, 0),
    ("qk", 3, 1), ("qk", 3, 2), ("qk", 3, 3), ("done", 4),
)


def make_kernel(planes, heads):
    rows_all = heads * ROWS
    group = 4
    grow = group * ROWS
    groups = heads // group
    ids = {}

    def kernel(lat_hbm, q_hbm, wk_hbm, wv_hbm, wn_hbm, seg_hbm, att_hbm, next_hbm,
               lat, seg, qv, wk, wv, wn, qx, kx, sc, top, ob, att, proj, part, rsa, rsb, nla, nlb,
               ls, ss, rs, ready):
        s = lax.axis_index("section")
        t = lax.axis_index("ctx")
        y = lax.axis_index("head")
        z, xh, c = t // 4, (t // 2) % 2, t % 2

        def at(zz, xx, cc, yy, section=s):
            return {"section": section, "ctx": zz * 4 + xx * 2 + cc, "head": yy}

        right, left, across = (y + 1) % 4, (y + 3) % 4, (y + 2) % 4

        def load(i, src, dst):
            return pltpu.make_async_copy(src, dst, ls.at[i])

        loads = [
            load(0, lat_hbm.at[0], lat),
            load(1, seg_hbm, seg),
            load(2, q_hbm.at[0], qv),
            load(3, wk_hbm.at[0], wk),
            load(4, wv_hbm.at[0], wv),
            load(5, wn_hbm.at[0], wn),
        ]
        for one in loads:
            one.start()

        barrier = pltpu.get_barrier_semaphore()
        peers = [at(z, xh, 1 - c, y), at(z, 1 - xh, c, y)]
        peers += [at(z, xx, c, yy) for xx in (xh, 1 - xh) for yy in (right, left, across)]
        peers += [at(z, xh, c, (y + d) % 4, 1 - s) for d in range(4)]
        for peer in peers:
            pl.semaphore_signal(barrier, inc=1, device_id=peer, device_id_type=MESH)
        for k in (1, 2):

            @pl.when(z + k < planes)
            def _():
                pl.semaphore_signal(barrier, inc=1, device_id=at((z + k) % planes, xh, c, y), device_id_type=MESH)

        @pl.when(z >= 1)
        def _():
            pl.semaphore_signal(barrier, inc=1, device_id=at((z + planes - 1) % planes, xh, c, y), device_id_type=MESH)

        def remote(name, src, dst, peer):
            i = ids.setdefault(name, len(ids))
            return pltpu.make_async_remote_copy(
                src_ref=src, dst_ref=dst, send_sem=ss.at[i], recv_sem=rs.at[i], device_id=peer, device_id_type=MESH
            )

        sent = []

        def send(name, src, dst, peer, when=None):
            one = remote(name, src, dst, peer)
            if when is None:
                one.start()
            else:
                pl.when(when)(one.start)
            sent.append((when, one))

        def arrive(name, dst, when=None):
            wait = remote(name, dst, dst, at(z, xh, c, right)).wait_recv
            if when is None:
                wait()
            else:
                pl.when(when)(wait)

        def start_of(k, cc, xx, yy=0):
            return pl.multiple_of(ROWS + CHUNK * (k - 1) + cc * 256 + xx * ROWS + yy * QUARTER, QUARTER)

        def block(k, cc, xx):
            return kx.at[pl.ds(start_of(k, cc, xx), ROWS)]

        def piece(k, xx, yy):
            return kx.at[pl.ds(start_of(k, c, xx, yy), QUARTER)]

        def beside(yy):
            return at(z, xh, c, yy)

        partner, twin = at(z, 1 - xh, c, y), at(z, xh, 1 - c, y)
        own = kx.at[pl.ds(0, ROWS)]
        own_piece = kx.at[pl.ds(pl.multiple_of(y * QUARTER, QUARTER), QUARTER)]

        loads[0].wait()
        loads[1].wait()
        lane = lax.broadcasted_iota(jnp.int32, (ROWS, 128), 1)
        docs = jnp.broadcast_to(seg[...], (ROWS, 128))
        line = lax.broadcasted_iota(jnp.int32, (ROWS, 128), 0)
        mine = jnp.where(line[0:ROPE, :] == docs[0:ROPE, :], 1.0, 0.0)
        kx[0:ROWS, :] = jnp.concatenate([lat[...].astype(F32), mine], axis=0).T.astype(BF16)
        in_slot = (line >= ROPE) & (line < ROPE + DOCS)
        q_mark = jnp.where(in_slot & (line - ROPE != docs), -BIG, 0.0).T
        pl.semaphore_wait(barrier, len(peers) + jnp.minimum(z, 2) + jnp.minimum(planes - 1 - z, 1))
        @pl.when(z >= 2)
        def _():
            pl.semaphore_signal(ready, inc=1, device_id=at((z + planes - 2) % planes, xh, c, y), device_id_type=MESH)

        def depart(k):
            send(("z", k), own_piece, piece(k, xh, y), at((z + k) % planes, xh, c, y), z + k < planes)

        def stage_z(k):
            arrive(("z", k), piece(k, xh, y), z >= k)

            @pl.when(z < k)
            def _():
                mark = lax.broadcasted_iota(jnp.int32, (QUARTER, 128), 1)
                mark = jnp.where((mark >= ROPE) & (mark < ROPE + DOCS), 1.0, 0.0)
                kx[pl.ds(start_of(k, c, xh, y), QUARTER), :] = jnp.concatenate(
                    [jnp.zeros((QUARTER, RANK), F32), mark], axis=1
                ).astype(BF16)

            mine = piece(k, xh, y)
            if k <= 2:
                send(
                    ("z", k + 2), mine, piece(k + 2, xh, y), at((z + 2) % planes, xh, c, y),
                    (z >= k) & (z + 2 < planes),
                )
            send(("x", k, 0), mine, mine, partner, xh == 1 if k == CHUNKS else None)
            for d in (1, 3, 2):
                send(("y", k, d), mine, mine, at(z, xh, c, (y + d) % 4))
            if ROUTES[k] == "S":
                for d in (1, 3, 2):
                    send(("x", k, d), mine, mine, at(z, 1 - xh, c, (y + d) % 4), xh == 1 if k == CHUNKS else None)

        def stage_x(k):
            far = xh == 0 if k == CHUNKS else None
            mine = piece(k, 1 - xh, y)
            arrive(("x", k, 0), mine, far)
            for d in (1, 3, 2):
                send(("y2", k, d), mine, mine, at(z, xh, c, (y + d) % 4), far)

        def stage_xs(k, d):
            mine = piece(k, xh, (y + 4 - d) % 4)
            arrive(("y", k, d), mine)
            send(("x", k, d), mine, mine, partner, xh == 1 if k == CHUNKS else None)

        def stage_ca(k):
            if ROUTES[k] != "X":
                for d in (1, 3, 2):
                    arrive(("y", k, d), piece(k, xh, (y + 4 - d) % 4))
            here = block(k, c, xh)
            send(("ca", k), here, here, twin, c == 1 if k == CHUNKS else None)

        def stage_cb(k):
            far = xh == 0 if k == CHUNKS else None
            if ROUTES[k] == "D":
                for d in (1, 3, 2):
                    arrive(("y2", k, d), piece(k, 1 - xh, (y + 4 - d) % 4), far)
            else:
                for d in range(4):
                    arrive(("x", k, d), piece(k, 1 - xh, (y + 4 - d) % 4 if d else y), far)
            here = block(k, c, 1 - xh)
            if k == CHUNKS:
                arrive("own", here, xh == 1)
            send(("cb", k), here, here, twin)

        def stage_done(k):
            arrive(("ca", k), block(k, 1 - c, xh))
            arrive(("cb", k), block(k, 1 - c, 1 - xh))

        def queries(p):
            base = 3 * 128 * p
            one = qv[:, base : base + 128]
            two = qv[:, base + 128 : base + 256].astype(F32)
            three = qv[:, base + 256 : base + 384].astype(F32)
            two_turned = pltpu.roll(two, 64, 1)
            three_turned = pltpu.roll(three, 64, 1)
            second = jnp.where(lane < 64, two_turned, three_turned).astype(BF16)
            for h, nope, pos in ((2 * p, one, two), (2 * p + 1, second, three_turned)):
                absorbed = lax.dot_general(
                    nope, wk[:, h * NOPE : (h + 1) * NOPE], NT, preferred_element_type=F32
                )
                qx[h * ROWS : (h + 1) * ROWS, 0:RANK] = (absorbed * FOLD).astype(BF16)
                qx[h * ROWS : (h + 1) * ROWS, RANK:WIDE] = jnp.where(lane < ROPE, pos * FOLD, q_mark).astype(BF16)

        def lane_max(scores):
            best = scores[:, 0:128]
            for i in range(1, scores.shape[1] // 128):
                best = jnp.maximum(best, scores[:, i * 128 : (i + 1) * 128])
            return best

        later = lax.broadcasted_iota(jnp.int32, (ROWS, ROWS), 1) > lax.broadcasted_iota(jnp.int32, (ROWS, ROWS), 0)
        causal = jnp.concatenate([jnp.where(later, -2.0 * BIG, 0.0)] * group, axis=0)

        def diagonal(g):
            r = slice(g * grow, (g + 1) * grow)
            scores = lax.dot_general(qx[r, :], kx[0:ROWS, :], NT, preferred_element_type=F32) + causal
            sc[r, 0:ROWS] = scores
            top[r, :] = scores

        def chunk_scores(k, g):
            r = slice(g * grow, (g + 1) * grow)
            first = ROWS + CHUNK * (k - 1)
            scores = lax.dot_general(qx[r, :], kx[first : first + CHUNK, :], NT, preferred_element_type=F32)
            sc[r, first : first + CHUNK] = scores
            top[r, :] = jnp.maximum(top[r, :], lane_max(scores))

        def lane_sum(weights):
            total = weights[:, 0:128]
            for i in range(1, weights.shape[1] // 128):
                total = total + weights[:, i * 128 : (i + 1) * 128]
            return total

        def finish(g):
            r = slice(g * grow, (g + 1) * grow)
            first = KEYS - CHUNK
            last = lax.dot_general(qx[r, :], kx[first:KEYS, :], NT, preferred_element_type=F32)
            high = jnp.max(jnp.maximum(top[r, :], lane_max(last)), axis=1, keepdims=True)
            early = jnp.exp2(sc[r, :] - high)
            late = jnp.exp2(last - high)
            total = jnp.sum(lane_sum(early) + lane_sum(late), axis=1, keepdims=True)
            mixed = jnp.dot(early.astype(BF16), kx[0:first, 0:RANK], preferred_element_type=F32)
            mixed = mixed + jnp.dot(late.astype(BF16), kx[first:KEYS, 0:RANK], preferred_element_type=F32)
            ob[r, :] = (mixed * (1.0 / total)).astype(BF16)
            for h in range(g * group, (g + 1) * group):
                att[:, h * VDIM : (h + 1) * VDIM] = jnp.dot(
                    ob[h * ROWS : (h + 1) * ROWS, :],
                    wv[:, h * VDIM : (h + 1) * VDIM],
                    preferred_element_type=F32,
                ).astype(BF16)
            mine = slice(g * group * VDIM, (g + 1) * group * VDIM)
            add = lax.dot_general(att[:, mine], wn[:, mine], NT, preferred_element_type=F32)
            if g == 0:
                proj[...] = add
            elif g < groups - 1:
                proj[...] += add
            else:
                total = proj[...] + add
                proj[...] = total
                part[...] = total.astype(BF16)

        depart(1)

        @pl.when(z + 2 < planes)
        def _():
            pl.semaphore_wait(ready, 1)

        when, first = sent.pop()
        pl.when(when)(first.wait_send)
        depart(2)
        send("own", own, block(CHUNKS, c, xh), partner, xh == 0)
        send(("ca", CHUNKS), own, block(CHUNKS, c, xh), twin, c == 0)
        loads[2].wait()
        loads[3].wait()
        steps = {
            "z": stage_z, "x": stage_x, "xs": stage_xs, "ca": stage_ca, "cb": stage_cb, "done": stage_done,
            "q": queries, "diag": diagonal, "qk": chunk_scores,
        }
        for step in PLAN:
            steps[step[0]](*step[1:])
        loads[4].wait()
        loads[5].wait()
        for g in range(groups):
            finish(g)
        store = pltpu.make_async_copy(att, att_hbm, ls.at[6])
        store.start()

        def sixteen(ref, yy, lower):
            return ref.at[pl.ds(pl.multiple_of(yy * QUARTER + lower * HALF, HALF), HALF)]

        for d in range(4):
            to = (y + d) % 4
            send(("rb", d), sixteen(part, to, 1), rsb.at[d], at(z, xh, c, to, 1 - s))
        for d in range(1, 4):
            to = (y + d) % 4
            send(("ra", d), sixteen(part, to, 0), rsa.at[d - 1], beside(to))

        def normal(total):
            low = total[:, 0:RANK]
            inverse = lax.rsqrt(jnp.sum(low * low, axis=1, keepdims=True) * (1.0 / RANK) + 1e-06)
            return (low * inverse).astype(BF16), total[:, RANK:LAT].astype(BF16)

        total = proj[pl.ds(pl.multiple_of(y * QUARTER, QUARTER), HALF), :]
        for d in range(1, 4):
            arrive(("ra", d), rsa.at[d - 1])
            total = total + rsa[d - 1].astype(F32)
        nla[:, 0:RANK], nla[:, RANK:LAT] = normal(total)
        for d in range(4):
            send(("na", d), nla, sixteen(nlb, y, 0), at(z, xh, c, (y + d) % 4, 1 - s))
        total = None
        for d in range(4):
            arrive(("rb", d), rsb.at[d])
            add = rsb[d].astype(F32)
            total = add if total is None else total + add
        lower = pl.ds(pl.multiple_of(y * QUARTER + HALF, HALF), HALF)
        nlb[lower, 0:RANK], nlb[lower, RANK:LAT] = normal(total)
        for d in range(1, 4):
            send(("nb", d), sixteen(nlb, y, 1), sixteen(nlb, y, 1), beside((y + d) % 4))
        for d in range(4):
            arrive(("na", d), sixteen(nlb, (y + 4 - d) % 4, 0))
        for d in range(1, 4):
            arrive(("nb", d), sixteen(nlb, (y + 4 - d) % 4, 1))
        out = pltpu.make_async_copy(nlb, next_hbm, ls.at[7])
        out.start()
        for when, one in sent:
            if when is None:
                one.wait_send()
            else:
                pl.when(when)(one.wait_send)
        store.wait()
        out.wait()

    def call(latent, queries, w_key, w_value, w_next, segments):
        return pl.pallas_call(
            kernel,
            out_shape=(
                jax.ShapeDtypeStruct((ROWS, heads * VDIM), BF16),
                jax.ShapeDtypeStruct((ROWS, LAT), BF16),
            ),
            in_specs=[pl.BlockSpec(memory_space=pl.ANY)] * 6,
            out_specs=[pl.BlockSpec(memory_space=pl.ANY)] * 2,
            scratch_shapes=[
                pltpu.VMEM((LAT, ROWS), BF16),
                pltpu.VMEM((1, ROWS), jnp.int32),
                pltpu.VMEM((ROWS, heads * (NOPE + ROPE)), BF16),
                pltpu.VMEM((RANK, heads * NOPE), BF16),
                pltpu.VMEM((RANK, heads * VDIM), BF16),
                pltpu.VMEM((LAT, heads * VDIM), BF16),
                pltpu.VMEM((rows_all, WIDE), BF16),
                pltpu.VMEM((KEYS, WIDE), BF16),
                pltpu.VMEM((rows_all, KEYS - CHUNK), F32),
                pltpu.VMEM((rows_all, 128), F32),
                pltpu.VMEM((rows_all, RANK), BF16),
                pltpu.VMEM((ROWS, heads * VDIM), BF16),
                pltpu.VMEM((ROWS, LAT), F32),
                pltpu.VMEM((ROWS, LAT), BF16),
                pltpu.VMEM((3, HALF, LAT), BF16),
                pltpu.VMEM((4, HALF, LAT), BF16),
                pltpu.VMEM((HALF, LAT), BF16),
                pltpu.VMEM((ROWS, LAT), BF16),
                pltpu.SemaphoreType.DMA((8,)),
                pltpu.SemaphoreType.DMA((SEMS,)),
                pltpu.SemaphoreType.DMA((SEMS,)),
                pltpu.SemaphoreType.REGULAR,
            ],
            compiler_params=pltpu.CompilerParams(
                collective_id=0, has_side_effects=True, vmem_limit_bytes=58 * 2**20
            ),
            name="attend",
        )(latent, queries, w_key, w_value, w_next, segments)

    return call


def hand_over(rows, turned, rows_out, turned_out):
    rows_out[0] = rows[...]
    turned_out[0] = turned[...].astype(F32).T.astype(BF16)


def results(rows, turned):
    return pl.pallas_call(
        hand_over,
        out_shape=(
            jax.ShapeDtypeStruct((1,) + rows.shape, BF16),
            jax.ShapeDtypeStruct((1, LAT, ROWS), BF16),
        ),
        name="results",
    )(rows, turned)


def solution(mesh):
    planes = mesh.shape["ctx"] // 4

    def local(latent, queries, w_key, w_value, w_next, segments):
        rows, mixed = make_kernel(planes, w_key.shape[2] // NOPE)(
            jnp.swapaxes(latent, 1, 2), queries, w_key, w_value, jnp.swapaxes(w_next, 1, 2), segments
        )
        attention, turned = results(rows, mixed)
        return attention, jnp.swapaxes(turned, 1, 2)

    in_specs = (
        P("section", "ctx", None),
        P("section", "ctx", "head"),
        P("section", None, "head"),
        P("section", None, "head"),
        P("section", "head", None),
        P("section", "ctx"),
    )
    out_specs = (P("section", "ctx", "head"), P("section", "ctx", None))
    return jax.shard_map(local, mesh=mesh, in_specs=in_specs, out_specs=out_specs, check_vma=False)
```

time: 70.2 us -> 53.8 us (0.77)
  the two profiles are of different devices: /device:TPU:2 before, /device:TPU:160 now
where the time goes in v2:
time: 53.8 us; the launch traced here: 53.6 us
  Pallas kernels  53 us (99%)
  between operations  0.64 us (1%)
    pallas_call x1, Pallas kernels, call(): pl.pallas_call(kernel, out_shape=(jax.ShapeDtypeStruct((ROWS, heads * VDI...  51 us
    pallas_call x1, Pallas kernels, results(): pl.pallas_call(hand_over, out_shape=(jax.ShapeDtypeStruct((1,) + rows.sha...  1.98 us

profile of v2, /device:TPU:160, one launch (start us, length us, event | category | flops | bytes accessed | tf_op | source)
XLA Modules:
  0.0 53.6 jit_solution(8107461545741115499)
XLA Ops:
  0.6 51.0 %attend.1 = (bf16[128,2048]{1,0:T(8,128)(2,1)}, bf16[128,576]{1,0:T(8,128)(2,1)}) custom-call(bf16[1,576,128]{2,1,0:T(8,128)(2,1)} %bitcast.4, bf16[1,128,3072]{2,1,0:T(8,128)(2,1)} %q_hbm.1, bf16[1,512,2048]{2,1,0:T(8,128)(2,1)} %wk_hbm.1, bf16[1,512,2048]{2,1,0:T(8,128)(2,1)} %wv_hbm.1, bf16[1,576,2048]{2,1,0:T(8,128)(2,1)} %bitcast.3, s32[1,128]{1,0:T(1,128)} %seg_hbm.1), custom_call_target="tpu_custom_call" | custom-call | tf_op jit(solution)/shard_map/attend/pallas_call | solution.py:350
  51.7 2.0 %results.1 = (bf16[1,128,2048]{2,1,0:T(8,128)(2,1)}, bf16[1,576,128]{2,1,0:T(8,128)(2,1)}) custom-call(bf16[128,2048]{1,0:T(8,128)(2,1)} %get-tuple-element.6.rows, bf16[128,576]{1,0:T(8,128)(2,1)} %get-tuple-element.7.turned), custom_call_target="tpu_custom_call" | custom-call | tf_op jit(solution)/shard_map/results/pallas_call | solution.py:397

commit v3 on v2

--- a/solution.py
+++ b/solution.py
@@ -16,6 +16,7 @@
 WIDE = 640
 ROWS = 128
 QUARTER = 32
+SPLIT = 2
 HALF = 16
 CHUNK = 512
 CHUNKS = 4
@@ -27,14 +28,15 @@
 F32 = jnp.float32
 BF16 = jnp.bfloat16
 SEMS = 72
-ROUTES = ('', 'X', 'D', 'X', 'S')
+ROUTES = ('', 'X', 'D', 'X', 'D')
 PLAN = (
-    ("q", 0), ("q", 1), ("q", 2), ("q", 3), ("q", 4), ("z", 1), ("q", 5), ("q", 6), ("q", 7), ("z", 2),
-    ("diag", 0), ("diag", 1), ("diag", 2), ("diag", 3), ("xs", 1, 1), ("xs", 1, 3), ("z", 3), ("xs", 1, 2),
-    ("ca", 1), ("x", 2), ("z", 4), ("ca", 2), ("xs", 3, 1), ("xs", 3, 3), ("xs", 3, 2), ("ca", 3), ("cb", 1),
-    ("cb", 2), ("done", 1), ("qk", 1, 0), ("qk", 1, 1), ("done", 2), ("qk", 1, 2), ("ca", 4), ("qk", 1, 3),
-    ("qk", 2, 0), ("cb", 4), ("qk", 2, 1), ("qk", 2, 2), ("qk", 2, 3), ("cb", 3), ("done", 3), ("qk", 3, 0),
-    ("qk", 3, 1), ("qk", 3, 2), ("qk", 3, 3), ("done", 4),
+    ("q", 0), ("q", 1), ("q", 2), ("q", 3), ("q", 4), ("q", 5), ("q", 6), ("z", 1), ("q", 7), ("diag", 0),
+    ("diag", 1), ("diag", 2), ("diag", 3), ("z", 2), ("xs", 1, 1), ("xs", 1, 3), ("xs", 1, 2), ("ca", 1),
+    ("z", 3), ("x", 2), ("ca", 2), ("cb", 1), ("z", 4), ("xs", 3, 1), ("xs", 3, 3), ("done", 1), ("xs", 3, 2),
+    ("ca", 3), ("qk", 1, 0), ("qk", 1, 1), ("qk", 1, 2), ("cb", 2), ("x", 4), ("qk", 1, 3), ("done", 2),
+    ("qk", 2, 0), ("ca", 4), ("qk", 2, 1), ("qk", 2, 2), ("cb", 3), ("qk", 2, 3), ("early", 0), ("cb", 4),
+    ("done", 3), ("early", 1), ("early", 2), ("early", 3), ("qk", 3, 0), ("qk", 3, 1), ("qk", 3, 2),
+    ("qk", 3, 3), ("done", 4),
 )
 
 
@@ -46,8 +48,8 @@
     ids = {}
 
     def kernel(lat_hbm, q_hbm, wk_hbm, wv_hbm, wn_hbm, seg_hbm, att_hbm, next_hbm,
-               lat, seg, qv, wk, wv, wn, qx, kx, sc, top, ob, att, proj, part, rsa, rsb, nla, nlb,
-               ls, ss, rs, ready):
+               lat, seg, qv, wk, wv, wn, qx, kx, sc, top, late_top, sums, acc, ob, att, proj, part, rsa, rsb, nla, nlb,
+               ls, ss, rs):
         s = lax.axis_index("section")
         t = lax.axis_index("ctx")
         y = lax.axis_index("head")
@@ -74,15 +76,13 @@
 
         barrier = pltpu.get_barrier_semaphore()
         peers = [at(z, xh, 1 - c, y), at(z, 1 - xh, c, y)]
-        peers += [at(z, xx, c, yy) for xx in (xh, 1 - xh) for yy in (right, left, across)]
+        peers += [at(z, xh, c, yy) for yy in (right, left, across)]
         peers += [at(z, xh, c, (y + d) % 4, 1 - s) for d in range(4)]
         for peer in peers:
             pl.semaphore_signal(barrier, inc=1, device_id=peer, device_id_type=MESH)
-        for k in (1, 2):
-
-            @pl.when(z + k < planes)
-            def _():
-                pl.semaphore_signal(barrier, inc=1, device_id=at((z + k) % planes, xh, c, y), device_id_type=MESH)
+        @pl.when(z + 1 < planes)
+        def _():
+            pl.semaphore_signal(barrier, inc=1, device_id=at((z + 1) % planes, xh, c, y), device_id_type=MESH)
 
         @pl.when(z >= 1)
         def _():
@@ -136,14 +136,7 @@
         kx[0:ROWS, :] = jnp.concatenate([lat[...].astype(F32), mine], axis=0).T.astype(BF16)
         in_slot = (line >= ROPE) & (line < ROPE + DOCS)
         q_mark = jnp.where(in_slot & (line - ROPE != docs), -BIG, 0.0).T
-        pl.semaphore_wait(barrier, len(peers) + jnp.minimum(z, 2) + jnp.minimum(planes - 1 - z, 1))
-        @pl.when(z >= 2)
-        def _():
-            pl.semaphore_signal(ready, inc=1, device_id=at((z + planes - 2) % planes, xh, c, y), device_id_type=MESH)
-
-        def depart(k):
-            send(("z", k), own_piece, piece(k, xh, y), at((z + k) % planes, xh, c, y), z + k < planes)
-
+        pl.semaphore_wait(barrier, len(peers) + jnp.minimum(z, 1) + jnp.minimum(planes - 1 - z, 1))
         def stage_z(k):
             arrive(("z", k), piece(k, xh, y), z >= k)
 
@@ -156,10 +149,10 @@
                 ).astype(BF16)
 
             mine = piece(k, xh, y)
-            if k <= 2:
+            if k < CHUNKS:
                 send(
-                    ("z", k + 2), mine, piece(k + 2, xh, y), at((z + 2) % planes, xh, c, y),
-                    (z >= k) & (z + 2 < planes),
+                    ("z", k + 1), mine, piece(k + 1, xh, y), at((z + 1) % planes, xh, c, y),
+                    (z >= k) & (z + 1 < planes),
                 )
             send(("x", k, 0), mine, mine, partner, xh == 1 if k == CHUNKS else None)
             for d in (1, 3, 2):
@@ -239,7 +232,13 @@
             first = ROWS + CHUNK * (k - 1)
             scores = lax.dot_general(qx[r, :], kx[first : first + CHUNK, :], NT, preferred_element_type=F32)
             sc[r, first : first + CHUNK] = scores
-            top[r, :] = jnp.maximum(top[r, :], lane_max(scores))
+            best = lane_max(scores)
+            if k <= SPLIT:
+                top[r, :] = jnp.maximum(top[r, :], best)
+            elif k == SPLIT + 1:
+                late_top[r, :] = best
+            else:
+                late_top[r, :] = jnp.maximum(late_top[r, :], best)
 
         def lane_sum(weights):
             total = weights[:, 0:128]
@@ -247,16 +246,34 @@
                 total = total + weights[:, i * 128 : (i + 1) * 128]
             return total
 
+        begin = ROWS + CHUNK * SPLIT
+
+        def early(g):
+            r = slice(g * grow, (g + 1) * grow)
+            high = jnp.max(top[r, :], axis=1, keepdims=True)
+            weights = jnp.exp2(sc[r, 0:begin] - high)
+            sums[r, :] = lane_sum(weights)
+            top[r, :] = jnp.broadcast_to(high, (grow, 128))
+            acc[r, :] = jnp.dot(weights.astype(BF16), kx[0:begin, 0:RANK], preferred_element_type=F32)
+
         def finish(g):
             r = slice(g * grow, (g + 1) * grow)
             first = KEYS - CHUNK
             last = lax.dot_general(qx[r, :], kx[first:KEYS, :], NT, preferred_element_type=F32)
-            high = jnp.max(jnp.maximum(top[r, :], lane_max(last)), axis=1, keepdims=True)
-            early = jnp.exp2(sc[r, :] - high)
+            best = lane_max(last)
+            if SPLIT < CHUNKS - 1:
+                best = jnp.maximum(best, late_top[r, :])
+            high = jnp.max(jnp.maximum(best, top[r, :]), axis=1, keepdims=True)
+            ratio = jnp.exp2(top[r, :] - high)
             late = jnp.exp2(last - high)
-            total = jnp.sum(lane_sum(early) + lane_sum(late), axis=1, keepdims=True)
-            mixed = jnp.dot(early.astype(BF16), kx[0:first, 0:RANK], preferred_element_type=F32)
+            total = sums[r, :] * ratio + lane_sum(late)
+            mixed = acc[r, :] * jnp.concatenate([ratio] * (RANK // 128), axis=1)
+            if SPLIT < CHUNKS - 1:
+                middle = jnp.exp2(sc[r, begin:first] - high)
+                total = total + lane_sum(middle)
+                mixed = mixed + jnp.dot(middle.astype(BF16), kx[begin:first, 0:RANK], preferred_element_type=F32)
             mixed = mixed + jnp.dot(late.astype(BF16), kx[first:KEYS, 0:RANK], preferred_element_type=F32)
+            total = jnp.sum(total, axis=1, keepdims=True)
             ob[r, :] = (mixed * (1.0 / total)).astype(BF16)
             for h in range(g * group, (g + 1) * group):
                 att[:, h * VDIM : (h + 1) * VDIM] = jnp.dot(
@@ -275,22 +292,14 @@
                 proj[...] = total
                 part[...] = total.astype(BF16)
 
-        depart(1)
-
-        @pl.when(z + 2 < planes)
-        def _():
-            pl.semaphore_wait(ready, 1)
-
-        when, first = sent.pop()
-        pl.when(when)(first.wait_send)
-        depart(2)
+        send(("z", 1), own_piece, piece(1, xh, y), at((z + 1) % planes, xh, c, y), z + 1 < planes)
         send("own", own, block(CHUNKS, c, xh), partner, xh == 0)
         send(("ca", CHUNKS), own, block(CHUNKS, c, xh), twin, c == 0)
         loads[2].wait()
         loads[3].wait()
         steps = {
             "z": stage_z, "x": stage_x, "xs": stage_xs, "ca": stage_ca, "cb": stage_cb, "done": stage_done,
-            "q": queries, "diag": diagonal, "qk": chunk_scores,
+            "q": queries, "diag": diagonal, "qk": chunk_scores, "early": early,
         }
         for step in PLAN:
             steps[step[0]](*step[1:])
@@ -366,6 +375,9 @@
                 pltpu.VMEM((KEYS, WIDE), BF16),
                 pltpu.VMEM((rows_all, KEYS - CHUNK), F32),
                 pltpu.VMEM((rows_all, 128), F32),
+                pltpu.VMEM((rows_all, 128), F32),
+                pltpu.VMEM((rows_all, 128), F32),
+                pltpu.VMEM((rows_all, RANK), F32),
                 pltpu.VMEM((rows_all, RANK), BF16),
                 pltpu.VMEM((ROWS, heads * VDIM), BF16),
                 pltpu.VMEM((ROWS, LAT), F32),
@@ -377,7 +389,6 @@
                 pltpu.SemaphoreType.DMA((8,)),
                 pltpu.SemaphoreType.DMA((SEMS,)),
                 pltpu.SemaphoreType.DMA((SEMS,)),
-                pltpu.SemaphoreType.REGULAR,
             ],
             compiler_params=pltpu.CompilerParams(
                 collective_id=0, has_side_effects=True, vmem_limit_bytes=58 * 2**20

time: 53.8 us -> 49.6 us (0.922)
  Pallas kernels: 53 us -> 48.3 us
    pallas_call x1, Pallas kernels: 51 us -> 46.3 us  [call(): pl.pallas_call(kernel, out_shape=(jax.ShapeDtypeStruct((ROWS, heads * VDI...]
where the time goes in v3:
time: 49.6 us; the launch traced here: 48.9 us
  Pallas kernels  48.3 us (97%)
  between operations  0.64 us (1%)
    pallas_call x1, Pallas kernels, call(): pl.pallas_call(kernel, out_shape=(jax.ShapeDtypeStruct((ROWS, heads * VDI...  46.3 us
    pallas_call x1, Pallas kernels, results(): pl.pallas_call(hand_over, out_shape=(jax.ShapeDtypeStruct((1,) + rows.sha...  1.98 us

profile of v3, /device:TPU:160, one launch (start us, length us, event | category | flops | bytes accessed | tf_op | source)
XLA Modules:
  0.0 48.9 jit_solution(8944460105891133165)
XLA Ops:
  0.6 46.3 %attend.1 = (bf16[128,2048]{1,0:T(8,128)(2,1)}, bf16[128,576]{1,0:T(8,128)(2,1)}) custom-call(bf16[1,576,128]{2,1,0:T(8,128)(2,1)} %bitcast.4, bf16[1,128,3072]{2,1,0:T(8,128)(2,1)} %q_hbm.1, bf16[1,512,2048]{2,1,0:T(8,128)(2,1)} %wk_hbm.1, bf16[1,512,2048]{2,1,0:T(8,128)(2,1)} %wv_hbm.1, bf16[1,576,2048]{2,1,0:T(8,128)(2,1)} %bitcast.3, s32[1,128]{1,0:T(1,128)} %seg_hbm.1), custom_call_target="tpu_custom_call" | custom-call | tf_op jit(solution)/shard_map/attend/pallas_call | solution.py:359
  47.0 2.0 %results.1 = (bf16[1,128,2048]{2,1,0:T(8,128)(2,1)}, bf16[1,576,128]{2,1,0:T(8,128)(2,1)}) custom-call(bf16[128,2048]{1,0:T(8,128)(2,1)} %get-tuple-element.6.rows, bf16[128,576]{1,0:T(8,128)(2,1)} %get-tuple-element.7.turned), custom_call_target="tpu_custom_call" | custom-call | tf_op jit(solution)/shard_map/results/pallas_call | solution.py:408

commit v4 on v3

--- a/solution.py
+++ b/solution.py
@@ -34,8 +34,8 @@
     ("diag", 1), ("diag", 2), ("diag", 3), ("z", 2), ("xs", 1, 1), ("xs", 1, 3), ("xs", 1, 2), ("ca", 1),
     ("z", 3), ("x", 2), ("ca", 2), ("cb", 1), ("z", 4), ("xs", 3, 1), ("xs", 3, 3), ("done", 1), ("xs", 3, 2),
     ("ca", 3), ("qk", 1, 0), ("qk", 1, 1), ("qk", 1, 2), ("cb", 2), ("x", 4), ("qk", 1, 3), ("done", 2),
-    ("qk", 2, 0), ("ca", 4), ("qk", 2, 1), ("qk", 2, 2), ("cb", 3), ("qk", 2, 3), ("early", 0), ("cb", 4),
-    ("done", 3), ("early", 1), ("early", 2), ("early", 3), ("qk", 3, 0), ("qk", 3, 1), ("qk", 3, 2),
+    ("qk", 2, 0), ("ca", 4), ("qk", 2, 1), ("qk", 2, 2), ("cb", 3), ("qk", 2, 3), ("early", 0), ("early", 1),
+    ("early", 2), ("early", 3), ("cb", 4), ("done", 3), ("qk", 3, 0), ("qk", 3, 1), ("qk", 3, 2),
     ("qk", 3, 3), ("done", 4),
 )
 

time: 49.6 us -> 48.8 us (0.984)
  Pallas kernels: 48.3 us -> 47.8 us
where the time goes in v4:
time: 48.8 us; the launch traced here: 48.5 us
  Pallas kernels  47.8 us (98%)
  between operations  0.64 us (1%)
    pallas_call x1, Pallas kernels, call(): pl.pallas_call(kernel, out_shape=(jax.ShapeDtypeStruct((ROWS, heads * VDI...  45.9 us
    pallas_call x1, Pallas kernels, results(): pl.pallas_call(hand_over, out_shape=(jax.ShapeDtypeStruct((1,) + rows.sha...  1.98 us

profile of v4, /device:TPU:160, one launch (start us, length us, event | category | flops | bytes accessed | tf_op | source)
XLA Modules:
  0.0 48.5 jit_solution(13584226695073455265)
XLA Ops:
  0.6 45.9 %attend.1 = (bf16[128,2048]{1,0:T(8,128)(2,1)}, bf16[128,576]{1,0:T(8,128)(2,1)}) custom-call(bf16[1,576,128]{2,1,0:T(8,128)(2,1)} %bitcast.4, bf16[1,128,3072]{2,1,0:T(8,128)(2,1)} %q_hbm.1, bf16[1,512,2048]{2,1,0:T(8,128)(2,1)} %wk_hbm.1, bf16[1,512,2048]{2,1,0:T(8,128)(2,1)} %wv_hbm.1, bf16[1,576,2048]{2,1,0:T(8,128)(2,1)} %bitcast.3, s32[1,128]{1,0:T(1,128)} %seg_hbm.1), custom_call_target="tpu_custom_call" | custom-call | tf_op jit(solution)/shard_map/attend/pallas_call | solution.py:359
  46.5 2.0 %results.1 = (bf16[1,128,2048]{2,1,0:T(8,128)(2,1)}, bf16[1,576,128]{2,1,0:T(8,128)(2,1)}) custom-call(bf16[128,2048]{1,0:T(8,128)(2,1)} %get-tuple-element.6.rows, bf16[128,576]{1,0:T(8,128)(2,1)} %get-tuple-element.7.turned), custom_call_target="tpu_custom_call" | custom-call | tf_op jit(solution)/shard_map/results/pallas_call | solution.py:408

commit v5 on v4

--- a/solution.py
+++ b/solution.py
@@ -256,8 +256,10 @@
             top[r, :] = jnp.broadcast_to(high, (grow, 128))
             acc[r, :] = jnp.dot(weights.astype(BF16), kx[0:begin, 0:RANK], preferred_element_type=F32)
 
+        wide = 2 * group
+
         def finish(g):
-            r = slice(g * grow, (g + 1) * grow)
+            r = slice(g * wide * ROWS, (g + 1) * wide * ROWS)
             first = KEYS - CHUNK
             last = lax.dot_general(qx[r, :], kx[first:KEYS, :], NT, preferred_element_type=F32)
             best = lane_max(last)
@@ -275,17 +277,17 @@
             mixed = mixed + jnp.dot(late.astype(BF16), kx[first:KEYS, 0:RANK], preferred_element_type=F32)
             total = jnp.sum(total, axis=1, keepdims=True)
             ob[r, :] = (mixed * (1.0 / total)).astype(BF16)
-            for h in range(g * group, (g + 1) * group):
+            for h in range(g * wide, (g + 1) * wide):
                 att[:, h * VDIM : (h + 1) * VDIM] = jnp.dot(
                     ob[h * ROWS : (h + 1) * ROWS, :],
                     wv[:, h * VDIM : (h + 1) * VDIM],
                     preferred_element_type=F32,
                 ).astype(BF16)
-            mine = slice(g * group * VDIM, (g + 1) * group * VDIM)
+            mine = slice(g * wide * VDIM, (g + 1) * wide * VDIM)
             add = lax.dot_general(att[:, mine], wn[:, mine], NT, preferred_element_type=F32)
             if g == 0:
                 proj[...] = add
-            elif g < groups - 1:
+            elif g < heads // wide - 1:
                 proj[...] += add
             else:
                 total = proj[...] + add
@@ -305,7 +307,7 @@
             steps[step[0]](*step[1:])
         loads[4].wait()
         loads[5].wait()
-        for g in range(groups):
+        for g in range(heads // wide):
             finish(g)
         store = pltpu.make_async_copy(att, att_hbm, ls.at[6])
         store.start()

time: 48.8 us -> 48.1 us (0.986)
  Pallas kernels: 47.8 us -> 47.2 us
    pallas_call x1, Pallas kernels: 45.9 us -> 45.2 us  [call(): pl.pallas_call(kernel, out_shape=(jax.ShapeDtypeStruct((ROWS, heads * VDI...]
where the time goes in v5:
time: 48.1 us; the launch traced here: 47.8 us
  Pallas kernels  47.2 us (98%)
  between operations  0.64 us (1%)
    pallas_call x1, Pallas kernels, call(): pl.pallas_call(kernel, out_shape=(jax.ShapeDtypeStruct((ROWS, heads * VDI...  45.2 us
    pallas_call x1, Pallas kernels, results(): pl.pallas_call(hand_over, out_shape=(jax.ShapeDtypeStruct((1,) + rows.sha...  1.98 us

profile of v5, /device:TPU:160, one launch (start us, length us, event | category | flops | bytes accessed | tf_op | source)
XLA Modules:
  0.0 47.8 jit_solution(13204223373795829401)
XLA Ops:
  0.6 45.2 %attend.1 = (bf16[128,2048]{1,0:T(8,128)(2,1)}, bf16[128,576]{1,0:T(8,128)(2,1)}) custom-call(bf16[1,576,128]{2,1,0:T(8,128)(2,1)} %bitcast.4, bf16[1,128,3072]{2,1,0:T(8,128)(2,1)} %q_hbm.1, bf16[1,512,2048]{2,1,0:T(8,128)(2,1)} %wk_hbm.1, bf16[1,512,2048]{2,1,0:T(8,128)(2,1)} %wv_hbm.1, bf16[1,576,2048]{2,1,0:T(8,128)(2,1)} %bitcast.3, s32[1,128]{1,0:T(1,128)} %seg_hbm.1), custom_call_target="tpu_custom_call" | custom-call | tf_op jit(solution)/shard_map/attend/pallas_call | solution.py:361
  45.9 2.0 %results.1 = (bf16[1,128,2048]{2,1,0:T(8,128)(2,1)}, bf16[1,576,128]{2,1,0:T(8,128)(2,1)}) custom-call(bf16[128,2048]{1,0:T(8,128)(2,1)} %get-tuple-element.6.rows, bf16[128,576]{1,0:T(8,128)(2,1)} %get-tuple-element.7.turned), custom_call_target="tpu_custom_call" | custom-call | tf_op jit(solution)/shard_map/results/pallas_call | solution.py:410
